TPU v7x, 32 devices: a whole 2x2x4 slice. The times are simulated.
32 devices in a mesh: branch: 2 (over core), seq: 4 (over y, x), rep: 4 (over z).
Axes of the slice: x: 2, y: 2, z: 4, core: 2. Of those that a mesh axis runs over, the one named last changes fastest.
Arguments:
- queries: bfloat16 [2, 2048, 2048], P('branch', ('rep', 'seq')), parts along dimension 1, may hold values from -64 to 64
- key_vecs: bfloat16 [2, 2048, 2048], P('branch', ('rep', 'seq')), parts along dimension 1, may hold values from -8 to 8
- value_vecs: bfloat16 [2, 2048, 2048], P('branch', ('rep', 'seq')), parts along dimension 1, may hold values from -6 to 6
- hidden_in: bfloat16 [2, 2048, 2048], P('branch', ('rep', 'seq')), parts along dimension 1, may hold values from -4 to 4
- out_proj: bfloat16 [2, 2048, 2048], P('branch', 'seq'), may hold values from -0.125 to 0.125
- couple_proj: bfloat16 [2, 2048, 2048], P('branch', 'seq'), may hold values from -0.125 to 0.125
- grad_mixed: bfloat16 [2, 2048, 2048], P('branch', ('rep', 'seq')), parts along dimension 1, may hold values from -6 to 6
Outputs:
- mixed_out: bfloat16 [2, 2048, 2048], P('branch', ('rep', 'seq')), parts along dimension 1
- grad_hidden: bfloat16 [2, 2048, 2048], P('branch', ('rep', 'seq')), parts along dimension 1
- grad_queries: bfloat16 [2, 2048, 2048], P('branch', ('rep', 'seq')), parts along dimension 1
- grad_keys: bfloat16 [2, 2048, 2048], P('branch', ('rep', 'seq')), parts along dimension 1
- grad_values: bfloat16 [2, 2048, 2048], P('branch', ('rep', 'seq')), parts along dimension 1
- grad_couple: float32 [2, 2048, 8192], P('branch', 'seq', 'rep'), parts along dimension 2
There are 4 independent parts, one for each index of `rep`. A program takes and returns all parts, laid end to end along the dimension named above; an argument that names none is the same for every part. Nothing has to cross between parts.
All inputs are finite; a program needn't handle non-finite values.
Results may differ from a plain program's by a relative error of at most 0.015.
Values may be sent and summed in bfloat16 or wider, within the bound.
A program may use at most 128 MiB of HBM per device.

v0:
```python
import math

import jax
import jax.numpy as jnp
from jax import lax
from jax.sharding import PartitionSpec as P

HEAD = 128


def swapped(value, axis, bit):
    mask = 2**bit
    pairs = [(source, source ^ mask) for source in range(lax.axis_size(axis))]
    return lax.ppermute(value, axis, pairs)


def contract(left, right, left_dim, right_dim):
    return lax.dot_general(
        left, right, (((left_dim,), (right_dim,)), ((), ())), preferred_element_type=jnp.float32
    )


def softmax_weights(query_item, key_item, factor):
    scores = contract(query_item, key_item, 1, 1) * factor
    row_max = jnp.max(scores, axis=-1, keepdims=True)
    raised = jnp.exp(scores - row_max)
    return raised / jnp.sum(raised, axis=-1, keepdims=True)


def forward_item(bundle, factor):
    query_item, key_item, value_item = bundle
    weights = softmax_weights(query_item, key_item, factor)
    return contract(weights.astype(jnp.bfloat16), value_item, 1, 0).astype(jnp.bfloat16)


def backward_item(bundle, factor):
    query_item, key_item, value_item, grad_item = bundle
    weights = softmax_weights(query_item, key_item, factor)
    weights_low = weights.astype(jnp.bfloat16)
    grad_weights = contract(grad_item, value_item, 1, 1)
    row_dot = jnp.sum(weights * grad_weights, axis=-1, keepdims=True)
    d_scores = (weights * (grad_weights - row_dot)).astype(jnp.bfloat16)
    grad_query = (contract(d_scores, key_item, 1, 0) * factor).astype(jnp.bfloat16)
    grad_key = (contract(d_scores, query_item, 0, 0) * factor).astype(jnp.bfloat16)
    grad_value = contract(weights_low, grad_item, 0, 0).astype(jnp.bfloat16)
    return (grad_query, grad_key, grad_value)


def head_items(block_rows, seq_len):
    groups = block_rows.shape[0] // seq_len
    heads_here = block_rows.shape[1] // HEAD
    return (
        block_rows.reshape(groups, seq_len, heads_here, HEAD)
        .transpose(0, 2, 1, 3)
        .reshape(groups * heads_here, seq_len, HEAD)
    )


def item_rows(items, groups):
    heads_here = items.shape[0] // groups
    seq_len = items.shape[1]
    return (
        items.reshape(groups, heads_here, seq_len, HEAD)
        .transpose(0, 2, 1, 3)
        .reshape(groups * seq_len, heads_here * HEAD)
    )


def on_device(queries, key_vecs, value_vecs, hidden_in, out_proj, couple_proj, grad_mixed):
    factor = 1.0 / math.sqrt(HEAD)
    tok_count = queries.shape[1]
    group_count = lax.axis_size("seq")
    seq_len = tok_count * group_count
    head_query, head_key, head_value = (
        lax.all_to_all(queries[0], "seq", split_axis=1, concat_axis=0, tiled=True),
        lax.all_to_all(key_vecs[0], "seq", split_axis=1, concat_axis=0, tiled=True),
        lax.all_to_all(value_vecs[0], "seq", split_axis=1, concat_axis=0, tiled=True),
    )
    groups = head_query.shape[0] // seq_len
    query_items = head_items(head_query, seq_len)
    key_items = head_items(head_key, seq_len)
    value_items = head_items(head_value, seq_len)
    attended_items = lax.map(
        lambda bundle: forward_item(bundle, factor), (query_items, key_items, value_items)
    )
    attended_rows = item_rows(attended_items, groups)
    out_local = out_proj[0]
    term = contract(attended_rows, out_local, 1, 0).astype(jnp.bfloat16)
    summed = hidden_in[0].astype(jnp.float32) + lax.psum_scatter(
        lax.optimization_barrier(term).astype(jnp.float32).astype(jnp.bfloat16),
        "seq",
        scatter_dimension=0,
        tiled=True,
    ).astype(jnp.float32)
    hidden = lax.optimization_barrier(summed.astype(jnp.bfloat16))
    partner = swapped(hidden, "branch", 0)
    couple_full = lax.all_gather(couple_proj, "seq", axis=1, tiled=True)[0]
    mixed_out = (hidden.astype(jnp.float32) + contract(partner, couple_full, 1, 0)).astype(
        jnp.bfloat16
    )
    grad_tok = grad_mixed[0]
    back_couple = contract(grad_tok, couple_full, 1, 1).astype(jnp.bfloat16)
    partner_back = swapped(back_couple, "branch", 0)
    grad_hid = (grad_tok.astype(jnp.float32) + partner_back.astype(jnp.float32)).astype(
        jnp.bfloat16
    )
    head_grad = contract(
        lax.all_gather(grad_hid, "seq", axis=0, tiled=True), out_local, 1, 1
    ).astype(jnp.bfloat16)
    grad_cpl = lax.psum_scatter(
        contract(partner, grad_tok, 0, 0).astype(jnp.bfloat16),
        "seq",
        scatter_dimension=0,
        tiled=True,
    ).astype(jnp.float32)
    grad_items = lax.map(
        lambda bundle: backward_item(bundle, factor),
        (query_items, key_items, value_items, head_items(head_grad, seq_len)),
    )
    back_rows = (
        item_rows(grad_items[0], groups),
        item_rows(grad_items[1], groups),
        item_rows(grad_items[2], groups),
    )
    grad_q, grad_k, grad_v = (
        lax.all_to_all(back_rows[0], "seq", split_axis=0, concat_axis=1, tiled=True),
        lax.all_to_all(back_rows[1], "seq", split_axis=0, concat_axis=1, tiled=True),
        lax.all_to_all(back_rows[2], "seq", split_axis=0, concat_axis=1, tiled=True),
    )
    return (
        mixed_out[None],
        grad_hid[None],
        grad_q[None],
        grad_k[None],
        grad_v[None],
        grad_cpl[None],
    )


def solution(mesh):
    return jax.shard_map(
        on_device,
        mesh=mesh,
        in_specs=(
            P("branch", ("rep", "seq"), None),
            P("branch", ("rep", "seq"), None),
            P("branch", ("rep", "seq"), None),
            P("branch", ("rep", "seq"), None),
            P("branch", "seq", None),
            P("branch", "seq", None),
            P("branch", ("rep", "seq"), None),
        ),
        out_specs=(
            P("branch", ("rep", "seq"), None),
            P("branch", ("rep", "seq"), None),
            P("branch", ("rep", "seq"), None),
            P("branch", ("rep", "seq"), None),
            P("branch", ("rep", "seq"), None),
            P("branch", "seq", "rep"),
        ),
        check_vma=False,
    )
```

profile of v0, /device:TPU:0, one launch (start us, length us, event | category | flops | bytes accessed | tf_op | source)
XLA Modules:
  0.0 300.5 jit_solution(9856916534792192745)
XLA Ops:
  9.6 5.2 %all-to-all-start = ((bf16[128,4,512]{2,0,1:T(8,128)(2,1)}), bf16[128,4,512]{2,0,1:T(8,128)(2,1)S(1)}, u32[]{:S(2)}, u32[]{:S(2)}) async-start(bf16[128,4,512]{2,0,1:T(8,128)(2,1)} %copy.28), calls=%async_computation | async-start | bytes 1048576 | tf_op jit(solution)/shard_map/all_to_all | solution.py:75
  17.1 5.7 %all-to-all-done = bf16[128,4,512]{2,0,1:T(8,128)(2,1)S(1)} async-done(((bf16[128,4,512]{2,0,1:T(8,128)(2,1)}), bf16[128,4,512]{2,0,1:T(8,128)(2,1)S(1)}, u32[]{:S(2)}, u32[]{:S(2)}) %all-to-all-start) | async-done | bytes 524320 | tf_op jit(solution)/shard_map/all_to_all | solution.py:75
  22.8 3.5 %all-to-all-start.1 = ((bf16[128,4,512]{2,0,1:T(8,128)(2,1)}), bf16[128,4,512]{2,0,1:T(8,128)(2,1)S(1)}, u32[]{:S(2)}, u32[]{:S(2)}) async-start(bf16[128,4,512]{2,0,1:T(8,128)(2,1)} %copy.29), calls=%async_computation.1 | async-start | bytes 1048576 | tf_op jit(solution)/shard_map/all_to_all | solution.py:76
  30.4 10.0 %all-to-all-done.1 = bf16[128,4,512]{2,0,1:T(8,128)(2,1)S(1)} async-done(((bf16[128,4,512]{2,0,1:T(8,128)(2,1)}), bf16[128,4,512]{2,0,1:T(8,128)(2,1)S(1)}, u32[]{:S(2)}, u32[]{:S(2)}) %all-to-all-start.1) | async-done | bytes 524320 | tf_op jit(solution)/shard_map/all_to_all | solution.py:76
  40.5 4.1 %all-to-all-start.2 = ((bf16[128,4,512]{2,0,1:T(8,128)(2,1)}), bf16[128,4,512]{2,0,1:T(8,128)(2,1)}, u32[]{:S(2)}, u32[]{:S(2)}) async-start(bf16[128,4,512]{2,0,1:T(8,128)(2,1)} %copy.30), calls=%async_computation.2 | async-start | bytes 1048576 | tf_op jit(solution)/shard_map/all_to_all | solution.py:77
  48.8 9.4 %all-to-all-done.2 = bf16[128,4,512]{2,0,1:T(8,128)(2,1)} async-done(((bf16[128,4,512]{2,0,1:T(8,128)(2,1)}), bf16[128,4,512]{2,0,1:T(8,128)(2,1)}, u32[]{:S(2)}, u32[]{:S(2)}) %all-to-all-start.2) | async-done | bytes 524320 | tf_op jit(solution)/shard_map/all_to_all | solution.py:77
  62.0 10.4 %while.24 = (s32[]{:T(128)}, bf16[4,512,128]{1,2,0:T(8,128)(2,1)}, bf16[4,512,128]{2,1,0:T(8,128)(2,1)S(1)}, bf16[4,512,128]{2,1,0:T(8,128)(2,1)S(1)}, bf16[4,512,128]{2,1,0:T(8,128)(2,1)}, /*index=5*/s32[]{:T(128)}) while((s32[]{:T(128)}, bf16[4,512,128]{1,2,0:T(8,128)(2,1)}, bf16[4,512,128]{2,1,0:T(8,128)(2,1)S(1)}, ...), condition=%wide.region_3.4_spmd, body=%wide.region_0.3_spmd.sunk | while | flops 136117248 | bytes 4206661 | solution.py:83
  72.4 3.6 %convolution_convert_fusion.3 = bf16[512,2048]{1,0:T(8,128)(2,1)} fusion(bf16[512,512]{0,1:T(8,128)(2,1)} %bitcast.175, bf16[1,512,2048]{2,1,0:T(8,128)(2,1)S(1)} %copy-done), kind=kOutput, calls=%fused_computation.58 | convolution fusion | flops 1074790400 | bytes 4718592 | tf_op jit(solution)/shard_map/dot_general | solution.py:18
  76.1 35.3 %all-gather.3.cloned.1.call-done = bf16[1,2048,2048]{2,1,0:T(8,128)(2,1)} async-done(((bf16[1,512,2048]{2,1,0:T(8,128)(2,1)}), bf16[1,2048,2048]{2,1,0:T(8,128)(2,1)}) %all-gather.3.cloned.1.call-update) | async-done | bytes 8388624 | tf_op jit(solution)/shard_map/all_gather | solution.py:97
  111.5 6.5 %fusion.49 = bf16[128,2048]{1,0:T(8,128)(2,1)S(1)} fusion(bf16[1,2048,2048]{2,1,0:T(8,128)(2,1)} %all-gather.3.cloned.1.call-done, bf16[1,128,2048]{2,1,0:T(8,128)(2,1)} %param.17), kind=kOutput, calls=%fused_computation.60 | convolution fusion | flops 1074003968 | bytes 9437184 | tf_op jit(solution)/shard_map/dot_general | solution.py:18
  121.1 29.1 %reduce-scatter.3.cloned.1.call-done = bf16[128,2048]{1,0:T(8,128)(2,1)} async-done(((bf16[512,2048]{1,0:T(8,128)(2,1)}), bf16[128,2048]{1,0:T(8,128)(2,1)}) %reduce-scatter.3.cloned.1.call-update) | async-done | bytes 524304 | tf_op jit(solution)/shard_map/reduce_scatter | solution.py:89
  155.1 6.7 %convolution_convert_fusion.2 = bf16[2048,2048]{1,0:T(8,128)(2,1)} fusion(bf16[128,2048]{1,0:T(8,128)(2,1)S(1)} %collective-permute-done, bf16[1,128,2048]{2,1,0:T(8,128)(2,1)} %param.17), kind=kOutput, calls=%fused_computation.57 | convolution fusion | flops 1077936128 | bytes 9437184 | tf_op jit(solution)/shard_map/dot_general | solution.py:18
  161.8 26.3 %all-gather.5.cloned.1.call-done = bf16[512,2048]{1,0:T(8,128)(2,1)} async-done(((bf16[128,2048]{1,0:T(8,128)(2,1)}), bf16[512,2048]{1,0:T(8,128)(2,1)}) %all-gather.5.cloned.1.call-update) | async-done | bytes 2097168 | tf_op jit(solution)/shard_map/all_gather | solution.py:108
  188.1 3.7 %fusion.61 = bf16[512,512]{0,1:T(8,128)(2,1)} fusion(bf16[512,2048]{1,0:T(8,128)(2,1)} %all-gather.5.cloned.1.call-done, bf16[1,512,2048]{2,1,0:T(8,128)(2,1)S(1)} %copy-done), kind=kOutput, calls=%fused_computation.67 | convolution fusion | flops 1074003968 | bytes 4718592 | tf_op jit(solution)/shard_map/dot_general | solution.py:18
  193.9 22.1 %while.25 = (s32[]{:T(128)}, bf16[4,512,128]{2,1,0:T(8,128)(2,1)}, bf16[4,512,128]{2,1,0:T(8,128)(2,1)}, bf16[4,512,128]{2,1,0:T(8,128)(2,1)}, bf16[4,512,128]{2...) while((s32[]{:T(128)}, bf16[4,512,128]{2,1,0:T(8,128)(2,1)}, ...), condition=%wide.region_9.10_spmd, body=%wide.region_5.9_spmd.sunk | while | flops 340064768 | bytes 12348537 | solution.py:116
  218.4 3.5 %all-to-all-start.3 = ((bf16[4,128,512]{2,1,0:T(8,128)(2,1)}), bf16[4,128,512]{2,1,0:T(8,128)(2,1)S(1)}, u32[]{:S(2)}, u32[]{:S(2)}) async-start(bf16[4,128,512]{2,1,0:T(8,128)(2,1)} %all_to_all.81), calls=%async_computation.4 | async-start | bytes 1048576 | tf_op jit(solution)/shard_map/all_to_all | solution.py:126
  224.3 12.1 %all-to-all-done.3 = bf16[4,128,512]{2,1,0:T(8,128)(2,1)S(1)} async-done(((bf16[4,128,512]{2,1,0:T(8,128)(2,1)}), bf16[4,128,512]{2,1,0:T(8,128)(2,1)S(1)}, u32[]{:S(2)}, u32[]{:S(2)}) %all-to-all-start.3) | async-done | bytes 524320 | tf_op jit(solution)/shard_map/all_to_all | solution.py:126
  236.4 4.1 %all-to-all-start.4 = ((bf16[4,128,512]{2,1,0:T(8,128)(2,1)}), bf16[4,128,512]{2,1,0:T(8,128)(2,1)}, u32[]{:S(2)}, u32[]{:S(2)}) async-start(bf16[4,128,512]{2,1,0:T(8,128)(2,1)} %all_to_all.84), calls=%async_computation.5 | async-start | bytes 1048576 | tf_op jit(solution)/shard_map/all_to_all | solution.py:127
  240.6 2.3 copy.43
  245.0 10.0 %all-to-all-done.4 = bf16[4,128,512]{2,1,0:T(8,128)(2,1)} async-done(((bf16[4,128,512]{2,1,0:T(8,128)(2,1)}), bf16[4,128,512]{2,1,0:T(8,128)(2,1)}, u32[]{:S(2)}, u32[]{:S(2)}) %all-to-all-start.4) | async-done | bytes 524320 | tf_op jit(solution)/shard_map/all_to_all | solution.py:127
  255.0 4.2 %all-to-all-start.5 = ((bf16[4,128,512]{2,1,0:T(8,128)(2,1)}), bf16[4,128,512]{2,1,0:T(8,128)(2,1)}, u32[]{:S(2)}, u32[]{:S(2)}) async-start(bf16[4,128,512]{2,1,0:T(8,128)(2,1)} %all_to_all.87), calls=%async_computation.6 | async-start | bytes 1048576 | tf_op jit(solution)/shard_map/all_to_all | solution.py:128
  259.2 5.5 %fusion.55 = bf16[1,128,2048]{2,1,0:T(8,128)(2,1)} fusion(bf16[128,2048]{1,0:T(8,128)(2,1)S(1)} %copy-done.3, bf16[1,2048,2048]{2,1,0:T(8,128)(2,1)} %all-gather.3.cloned.1.call-done, bf16[128,2048]{1,0:T(8,128)(2,1)} %copy-done.4), kind=kOutput, calls=%fused_computation.62 | convolution fusion | flops 1074528256 | bytes 9961472 | tf_op jit(solution)/shard_map/dot_general | solution.py:18
  270.6 19.2 %reduce-scatter.5.cloned.1.call-done = bf16[512,2048]{1,0:T(8,128)(2,1)} async-done(((bf16[2048,2048]{1,0:T(8,128)(2,1)}), bf16[512,2048]{1,0:T(8,128)(2,1)}) %reduce-scatter.5.cloned.1.call-update) | async-done | bytes 2097168 | tf_op jit(solution)/shard_map/reduce_scatter | solution.py:110
  289.8 4.1 %bitcast_convert_fusion = f32[1,512,2048]{2,1,0:T(8,128)} fusion(bf16[512,2048]{1,0:T(8,128)(2,1)} %reduce-scatter.5.cloned.1.call-done), kind=kLoop, calls=%fused_computation.63 | loop fusion | flops 1048576 | bytes 6291456 | tf_op jit(solution)/shard_map/broadcast_in_dim | solution.py:136
  (111 shorter events, 72.2 us)
Async XLA Ops:
  7.2 65.2 %copy-start = (bf16[1,512,2048]{2,1,0:T(8,128)(2,1)S(1)}, bf16[1,512,2048]{2,1,0:T(8,128)(2,1)}, u32[]{:S(2)}) copy-start(bf16[1,512,2048]{2,1,0:T(8,128)(2,1)} %param.15) | copy-start | bytes 6291460
  7.2 1.2 copy-start.5
  7.2 104.3 %all-gather.3.cloned.1.call-start = ((), (), s32[]{:S(2)}) async-start(), calls=%async_computation.9 | async-start | bytes 10485760 | tf_op jit(solution)/shard_map/all_gather | solution.py:97
  9.6 13.2 %all-to-all-start = ((bf16[128,4,512]{2,0,1:T(8,128)(2,1)}), bf16[128,4,512]{2,0,1:T(8,128)(2,1)S(1)}, u32[]{:S(2)}, u32[]{:S(2)}) async-start(bf16[128,4,512]{2,0,1:T(8,128)(2,1)} %copy.28), calls=%async_computation | async-start | bytes 1048576 | tf_op jit(solution)/shard_map/all_to_all | solution.py:75
  22.8 17.7 %all-to-all-start.1 = ((bf16[128,4,512]{2,0,1:T(8,128)(2,1)}), bf16[128,4,512]{2,0,1:T(8,128)(2,1)S(1)}, u32[]{:S(2)}, u32[]{:S(2)}) async-start(bf16[128,4,512]{2,0,1:T(8,128)(2,1)} %copy.29), calls=%async_computation.1 | async-start | bytes 1048576 | tf_op jit(solution)/shard_map/all_to_all | solution.py:76
  40.5 17.6 %all-to-all-start.2 = ((bf16[128,4,512]{2,0,1:T(8,128)(2,1)}), bf16[128,4,512]{2,0,1:T(8,128)(2,1)}, u32[]{:S(2)}, u32[]{:S(2)}) async-start(bf16[128,4,512]{2,0,1:T(8,128)(2,1)} %copy.30), calls=%async_computation.2 | async-start | bytes 1048576 | tf_op jit(solution)/shard_map/all_to_all | solution.py:77
  44.6 105.6 %reduce-scatter.3.cloned.1.call-start = ((), (), s32[]{:S(2)}) async-start(), calls=%async_computation.8 | async-start | bytes 2621440 | tf_op jit(solution)/shard_map/reduce_scatter | solution.py:89
  76.1 112.1 %all-gather.5.cloned.1.call-start = ((), (), s32[]{:S(2)}) async-start(), calls=%async_computation.10 | async-start | bytes 2621440 | tf_op jit(solution)/shard_map/all_gather | solution.py:108
  111.5 8.5 %copy-start.1 = (bf16[1,128,2048]{2,1,0:T(8,128)(2,1)S(1)}, bf16[1,128,2048]{2,1,0:T(8,128)(2,1)}, u32[]{:S(2)}) copy-start(bf16[1,128,2048]{2,1,0:T(8,128)(2,1)} %param.17) | copy-start | bytes 1572868
  117.9 2.0 collective-permute-start.1
  120.9 169.0 %reduce-scatter.5.cloned.1.call-start = ((), (), s32[]{:S(2)}) async-start(), calls=%async_computation.11 | async-start | bytes 10485760 | tf_op jit(solution)/shard_map/reduce_scatter | solution.py:110
  151.6 0.8 copy-start.4
  152.4 1.9 collective-permute-start
  154.3 0.8 copy-start.2
  193.9 1.0 copy-start.6
  199.4 1.0 copy-start.6
  204.9 1.0 copy-start.6
  210.4 1.0 copy-start.6
  218.4 18.0 %all-to-all-start.3 = ((bf16[4,128,512]{2,1,0:T(8,128)(2,1)}), bf16[4,128,512]{2,1,0:T(8,128)(2,1)S(1)}, u32[]{:S(2)}, u32[]{:S(2)}) async-start(bf16[4,128,512]{2,1,0:T(8,128)(2,1)} %all_to_all.81), calls=%async_computation.4 | async-start | bytes 1048576 | tf_op jit(solution)/shard_map/all_to_all | solution.py:126
  224.3 34.8 %copy-start.3 = (bf16[128,2048]{1,0:T(8,128)(2,1)S(1)}, bf16[128,2048]{1,0:T(8,128)(2,1)}, u32[]{:S(2)}) copy-start(bf16[128,2048]{1,0:T(8,128)(2,1)} %copy-done.2) | copy-start | bytes 1572868
  236.4 18.6 %all-to-all-start.4 = ((bf16[4,128,512]{2,1,0:T(8,128)(2,1)}), bf16[4,128,512]{2,1,0:T(8,128)(2,1)}, u32[]{:S(2)}, u32[]{:S(2)}) async-start(bf16[4,128,512]{2,1,0:T(8,128)(2,1)} %all_to_all.84), calls=%async_computation.5 | async-start | bytes 1048576 | tf_op jit(solution)/shard_map/all_to_all | solution.py:127
  255.0 13.3 %all-to-all-start.5 = ((bf16[4,128,512]{2,1,0:T(8,128)(2,1)}), bf16[4,128,512]{2,1,0:T(8,128)(2,1)}, u32[]{:S(2)}, u32[]{:S(2)}) async-start(bf16[4,128,512]{2,1,0:T(8,128)(2,1)} %all_to_all.87), calls=%async_computation.6 | async-start | bytes 1048576 | tf_op jit(solution)/shard_map/all_to_all | solution.py:128
Sparse Core Ops, SparseCore 0:
  9.9 101.5 all-gather.2
  115.0 35.1 reduce-scatter.2
  152.8 35.2 all-gather.4
  191.3 98.4 reduce-scatter.4
where the time goes:
time: 302 us; the launch traced here: 301 us
  waiting for transfers between devices  162 us (54%)
  matrix products  50.4 us (17%)
  local copies, waits for them, and re-layouts  40.2 us (13%)
  starting transfers between devices  25 us (8%)
  between operations  13.9 us (5%)
  other arithmetic  9.09 us (3%)
    dot_general x33, matrix products, contract(): lax.dot_general(left, right, (((left_dim,), (right_dim,)), ((), ())), pre...  50.4 us
    all_gather x1, waiting for transfers between devices, on_device(): couple_full = lax.all_gather(couple_proj, 'seq', axis=1, tiled=True)[0]  35.3 us
    reduce_scatter x1, waiting for transfers between devices, on_device(): lax.psum_scatter(lax.optimization_barrier(term).astype(jnp.float32).astyp...  29.1 us
    all_gather x1, waiting for transfers between devices, on_device(): lax.all_gather(grad_hid, 'seq', axis=0, tiled=True)  26.3 us
    reduce_scatter x1, waiting for transfers between devices, on_device(): lax.psum_scatter(contract(partner, grad_tok, 0, 0).astype(jnp.bfloat16),...  19.2 us
    all_to_all x1, waiting for transfers between devices, on_device(): lax.all_to_all(back_rows[0], 'seq', split_axis=0, concat_axis=1, tiled=True)  12.1 us
    all_to_all x1, waiting for transfers between devices, on_device(): lax.all_to_all(back_rows[1], 'seq', split_axis=0, concat_axis=1, tiled=True)  10 us
    all_to_all x1, waiting for transfers between devices, on_device(): lax.all_to_all(key_vecs[0], 'seq', split_axis=1, concat_axis=0, tiled=True)  10 us
  transfers between devices with their start and end apart: 12, of which 11 were waited for; matrix products, arithmetic and copies ran while one was open for 28% of the time, Pallas kernels for 0%

commit v1 on v0

v1 whole, which is shorter than its diff:
```python
import math

import jax
import jax.numpy as jnp
from jax import lax
from jax.sharding import PartitionSpec as P

HEAD = 128


def swapped(value, axis):
    pairs = [(source, source ^ 1) for source in range(lax.axis_size(axis))]
    return lax.ppermute(value, axis, pairs)


def contract(left, right, left_dim, right_dim):
    return lax.dot_general(
        left, right, (((left_dim,), (right_dim,)), ((), ())), preferred_element_type=jnp.float32
    )


def batched(left, right, left_dim, right_dim):
    return lax.dot_general(
        left, right, (((left_dim,), (right_dim,)), ((0,), (0,))), preferred_element_type=jnp.float32
    )


def heads(rows):
    return rows.reshape(rows.shape[0], -1, HEAD).transpose(1, 0, 2)


def rows_of(items):
    return items.transpose(1, 0, 2).reshape(items.shape[1], -1)


def on_device(queries, key_vecs, value_vecs, hidden_in, out_proj, couple_proj, grad_mixed):
    factor = 1.0 / math.sqrt(HEAD)
    bf16 = jnp.bfloat16
    tok = queries.shape[1]
    me = lax.axis_index("seq")
    wide = couple_proj.shape[1]
    out_local, couple = out_proj[0], couple_proj[0]
    gm_all = lax.all_gather(grad_mixed[0], "seq", axis=0, tiled=True)
    stacked = jnp.concatenate([queries, key_vecs, value_vecs], axis=0)
    moved = lax.all_to_all(stacked, "seq", split_axis=2, concat_axis=1, tiled=True)
    q, k, v = heads(moved[0]), heads(moved[1]), heads(moved[2])
    back = contract(gm_all, couple, 1, 1).astype(bf16)
    back_all = lax.all_gather(swapped(back, "branch"), "seq", axis=1, tiled=True)
    scores = batched(q, k, 2, 2) * factor
    raised = jnp.exp(scores - jnp.max(scores, axis=-1, keepdims=True))
    weights = raised / jnp.sum(raised, axis=-1, keepdims=True)
    weights_low = weights.astype(bf16)
    attended = rows_of(batched(weights_low, v, 2, 1).astype(bf16))
    term = contract(attended, out_local, 1, 0)
    mine = lax.dynamic_slice_in_dim(term, me * tok, tok, 0) + hidden_in[0].astype(jnp.float32)
    term = lax.dynamic_update_slice_in_dim(term, mine, me * tok, 0).astype(bf16)
    hidden = lax.psum_scatter(term, "seq", scatter_dimension=1, tiled=True)
    partner = swapped(hidden, "branch")
    mixed = contract(partner, couple, 1, 0)
    own = lax.dynamic_slice_in_dim(mixed, me * wide, wide, 1) + hidden.astype(jnp.float32)
    mixed = lax.dynamic_update_slice_in_dim(mixed, own, me * wide, 1).astype(bf16)
    mixed_out = lax.psum_scatter(mixed, "seq", scatter_dimension=0, tiled=True)
    grad_cpl = contract(partner, gm_all, 0, 0)
    grad_hid = (gm_all.astype(jnp.float32) + back_all.astype(jnp.float32)).astype(bf16)
    grad_mine = lax.dynamic_slice_in_dim(grad_hid, me * tok, tok, 0)
    head_grad = heads(contract(grad_hid, out_local, 1, 1).astype(bf16))
    grad_w = batched(head_grad, v, 2, 2)
    row_dot = jnp.sum(weights * grad_w, axis=-1, keepdims=True)
    d_scores = (weights * (grad_w - row_dot)).astype(bf16)
    gq = rows_of((batched(d_scores, k, 2, 1) * factor).astype(bf16))
    gk = rows_of((batched(d_scores, q, 1, 1) * factor).astype(bf16))
    gv = rows_of(batched(weights_low, head_grad, 1, 1).astype(bf16))
    out = lax.all_to_all(jnp.stack([gq, gk, gv]), "seq", split_axis=1, concat_axis=2, tiled=True)
    return (mixed_out[None], grad_mine[None], out[0:1], out[1:2], out[2:3], grad_cpl[None])


def solution(mesh):
    token = P("branch", ("rep", "seq"), None)
    weight = P("branch", "seq", None)
    return jax.shard_map(
        on_device,
        mesh=mesh,
        in_specs=(token, token, token, token, weight, weight, token),
        out_specs=(token, token, token, token, token, P("branch", "seq", "rep")),
        check_vma=False,
    )
```

time: 302 us -> 245 us (0.81)
  waiting for transfers between devices: 162 us -> 117 us
  matrix products: 50.4 us -> 31.7 us
  starting transfers between devices: 25 us -> 10.4 us
  local copies, waits for them, and re-layouts: 40.2 us -> 50.9 us
  other arithmetic: 9.09 us -> 19.5 us
    dot_general x33 -> x5, matrix products: 50.4 us -> 11.6 us  [contract(): lax.dot_general(left, right, (((left_dim,), (right_dim,)), ((), ())), pre...]
    all_gather x2, waiting for transfers between devices: 61.7 us -> 32.4 us  [the longest x1 32.4 us: on_device(): lax.all_gather(swapped(back, 'branch'), 'seq', axis=1, tiled=True)]
    slice x0 -> x8, local copies, waits for them, and re-layouts: none -> 21.5 us  [the longest x3 10.5 us: on_device(): out[2:3]]
    dot_general x0 -> x6, matrix products: none -> 20.1 us  [batched(): lax.dot_general(left, right, (((left_dim,), (right_dim,)), ((0,), (0,))),...]
    reduce_scatter x2, waiting for transfers between devices: 48.4 us -> 29.9 us  [the longest x1 29.9 us: on_device(): hidden = lax.psum_scatter(term, 'seq', scatter_dimension=1, tiled=True)]
    another operation x0 -> x7, local copies, waits for them, and re-layouts: none -> 15.3 us  [the longest x3 9.55 us: on_device(): jnp.stack([gq, gk, gv])]
    all_to_all x6 -> x2, starting transfers between devices: 24.6 us -> 9.97 us  [the longest x1 5.16 us: on_device(): lax.all_to_all(stacked, 'seq', split_axis=2, concat_axis=1, tiled=True)]
    all_to_all x12 -> x1, local copies, waits for them, and re-layouts: 14.6 us -> 4.09 us  [on_device(): lax.all_to_all(stacked, 'seq', split_axis=2, concat_axis=1, tiled=True)]
  transfers between devices with their start and end apart: 12 -> 8, of which waited for: 11 -> 6; matrix products, arithmetic and copies ran while one was open for 28% -> 37% of each run, Pallas kernels for 0% -> 0%
where the time goes in v1:
time: 245 us; the launch traced here: 244 us
  waiting for transfers between devices  117 us (48%)
  local copies, waits for them, and re-layouts  50.9 us (21%)
  matrix products  31.7 us (13%)
  other arithmetic  19.5 us (8%)
  between operations  14 us (6%)
  starting transfers between devices  10.4 us (4%)
    all_gather x1, waiting for transfers between devices, on_device(): lax.all_gather(swapped(back, 'branch'), 'seq', axis=1, tiled=True)  32.4 us
    all_to_all x1, waiting for transfers between devices, on_device(): lax.all_to_all(stacked, 'seq', split_axis=2, concat_axis=1, tiled=True)  30.6 us
    reduce_scatter x1, waiting for transfers between devices, on_device(): hidden = lax.psum_scatter(term, 'seq', scatter_dimension=1, tiled=True)  29.9 us
    dot_general x6, matrix products, batched(): lax.dot_general(left, right, (((left_dim,), (right_dim,)), ((0,), (0,))),...  20.1 us
    all_to_all x1, waiting for transfers between devices, on_device(): lax.all_to_all(jnp.stack([gq, gk, gv]), 'seq', split_axis=1, concat_axis=...  19.8 us
    dot_general x5, matrix products, contract(): lax.dot_general(left, right, (((left_dim,), (right_dim,)), ((), ())), pre...  11.6 us
    slice x3, local copies, waits for them, and re-layouts, on_device(): out[2:3]  10.5 us
    another operation x3, local copies, waits for them, and re-layouts, on_device(): jnp.stack([gq, gk, gv])  9.55 us
  transfers between devices with their start and end apart: 8, of which 6 were waited for; matrix products, arithmetic and copies ran while one was open for 37% of the time, Pallas kernels for 0%

profile of v1, /device:TPU:0, one launch (start us, length us, event | category | flops | bytes accessed | tf_op | source)
XLA Modules:
  0.0 244.0 jit_solution(6798783725134559623)
XLA Ops:
  7.2 2.8 %pad_maximum_fusion.1 = bf16[3,128,2048]{2,1,0:T(8,128)(2,1)} fusion(bf16[1,128,2048]{2,1,0:T(8,128)(2,1)} %param.9, bf16[1,128,2048]{2,1,0:T(8,128)(2,1)} %param.8, bf16[1,128,2048]{2,1,0:T(8,128)(2,1)} %param.7), kind=kLoop, calls=%fused_computation.21 | loop fusion | flops 1572864 | bytes 3145728 | tf_op jit(solution)/shard_map/concatenate | solution.py:44
  10.0 4.1 %copy.57 = bf16[3,128,2048]{1,0,2:T(4,128)(2,1)} copy(bf16[3,128,2048]{2,1,0:T(8,128)(2,1)} %pad_maximum_fusion.1) | data formatting | bytes 3145728 | tf_op jit(solution)/shard_map/concatenate | solution.py:44
  14.2 5.2 %all-to-all-start = ((bf16[3,128,2048]{1,0,2:T(4,128)(2,1)}), bf16[3,128,2048]{1,0,2:T(4,128)(2,1)}, u32[]{:S(2)}, u32[]{:S(2)}) async-start(bf16[3,128,2048]{1,0,2:T(4,128)(2,1)} %copy.57), calls=%async_computation | async-start | bytes 4194304 | tf_op jit(solution)/shard_map/all_to_all | solution.py:45
  20.1 30.6 %all-to-all-done = bf16[3,128,2048]{1,0,2:T(4,128)(2,1)} async-done(((bf16[3,128,2048]{1,0,2:T(4,128)(2,1)}), bf16[3,128,2048]{1,0,2:T(4,128)(2,1)}, u32[]{:S(2)}, u32[]{:S(2)}) %all-to-all-start) | async-done | bytes 1572896 | tf_op jit(solution)/shard_map/all_to_all | solution.py:45
  50.7 4.1 %copy.58 = bf16[3,128,4,512]{3,1,2,0:T(8,128)(2,1)} copy(bf16[3,128,4,512]{1,0,3,2:T(4,128)(2,1)} %bitcast) | data formatting | bytes 3145728 | tf_op jit(solution)/shard_map/all_to_all | solution.py:45
  54.8 2.5 %fusion.50 = (bf16[1,4,128,512]{3,2,1,0:T(8,128)(2,1)S(1)}, bf16[1,4,128,512]{3,2,1,0:T(8,128)(2,1)}, bf16[1,4,128,512]{3,2,1,0:T(8,128)(2,1)}) fusion(bf16[3,4,128,512]{3,2,1,0:T(8,128)(2,1)} %bitcast.87), kind=kLoop, calls=%fused_computation.50 | loop fusion | bytes 3145728 | tf_op jit(solution)/shard_map/slice | solution.py:46
  63.7 3.4 %fusion.51 = (f32[4,512]{1,0:T(4,128)S(1)}, f32[4,512,512]{1,2,0:T(8,128)}) fusion(f32[4,512,512]{1,2,0:T(8,128)S(1)} %fusion.32), kind=kOutput, calls=%fused_computation.51 | output fusion | flops 4194815 | bytes 8396800 | tf_op jit(solution)/shard_map/sub | solution.py:50
  67.1 5.2 %convolution_convert_fusion = bf16[4,512,128]{1,2,0:T(8,128)(2,1)S(1)} fusion(bf16[512,4,128]{0,2,1:T(8,128)(2,1)} %copy.84, f32[4,512]{1,0:T(4,128)S(1)} %get-tuple-element.12, f32[4,512,512]{1,2,0:T(8,128)} %copy-done.3), kind=kOutput, calls=%fused_computation.26 | convolution fusion | flops 273943040 | bytes 5251072 | tf_op jit(solution)/shard_map/dot_general | solution.py:23
  72.4 2.9 %fusion.12 = f32[512,2048]{1,0:T(8,128)S(1)} fusion(bf16[512,512]{0,1:T(8,128)(2,1)S(1)} %bitcast.91, bf16[1,512,2048]{2,1,0:T(8,128)(2,1)} %param.11), kind=kOutput, calls=%fused_computation.17 | convolution fusion | flops 1073741824 | bytes 6815744 | tf_op jit(solution)/shard_map/dot_general | solution.py:17
  77.3 2.9 %fusion.18 = bf16[512,512]{1,0:T(8,128)(2,1)S(1)} fusion(bf16[1,512,2048]{2,1,0:T(8,128)(2,1)S(1)} %copy-done, bf16[1,512,2048]{2,1,0:T(8,128)(2,1)} %all-gather.6.cloned.1.call-done), kind=kOutput, calls=%fused_computation.25 | convolution fusion | flops 1074003968 | bytes 4718592 | tf_op jit(solution)/shard_map/dot_general | solution.py:17
  83.2 29.9 %reduce-scatter.3.cloned.1.call-done = bf16[512,512]{1,0:T(8,128)(2,1)} async-done(((bf16[512,2048]{1,0:T(8,128)(2,1)}), bf16[512,512]{1,0:T(8,128)(2,1)}) %reduce-scatter.3.cloned.1.call-update) | async-done | bytes 524304 | tf_op jit(solution)/shard_map/reduce_scatter | solution.py:57
  118.4 32.4 %all-gather.4.cloned.1.call-done = bf16[512,2048]{1,0:T(8,128)(2,1)} async-done(((bf16[512,512]{1,0:T(8,128)(2,1)}), bf16[512,2048]{1,0:T(8,128)(2,1)}) %all-gather.4.cloned.1.call-update) | async-done | bytes 2097168 | tf_op jit(solution)/shard_map/all_gather | solution.py:48
  150.8 2.5 %add_convert_fusion = bf16[512,2048]{1,0:T(8,128)(2,1)S(1)} fusion(bf16[512,2048]{1,0:T(8,128)(2,1)} %all-gather.4.cloned.1.call-done, bf16[1,512,2048]{2,1,0:T(8,128)(2,1)S(1)} %copy-done.4), kind=kLoop, calls=%fused_computation.3 | loop fusion | flops 4194304 | bytes 6291456 | tf_op jit(solution)/shard_map/convert_element_type | solution.py:64
  156.0 6.0 %convolution_convert_fusion.1 = bf16[4,512,128]{1,2,0:T(8,128)(2,1)} fusion(bf16[4,512,128]{1,2,0:T(8,128)(2,1)S(1)} %bitcast.93, f32[4,512]{1,0:T(4,128)S(1)} %get-tuple-element.12, f32[4,512,512]{1,2,0:T(8,128)} %copy-done.3), kind=kOutput, calls=%fused_computation.27 | convolution fusion | flops 273943040 | bytes 5251072 | tf_op jit(solution)/shard_map/dot_general | solution.py:23
  164.4 3.6 %multiply_reduce_fusion = (f32[4,512]{1,0:T(4,128)S(1)}, f32[4,512,512]{1,2,0:T(8,128)S(1)}) fusion(f32[4,512,512]{1,2,0:T(8,128)} %get-tuple-element.13, f32[4,512]{1,0:T(4,128)S(1)} %get-tuple-element.12, bf16[4,512,128]{1,2,0:T(8,128)(2,1)} %bitcast.94, bf16[512,4,128]{0,2,1:T(8,128)(2,1)} %copy.84), kind=kOutput, calls=%fused_computation.2 | convolution fusion | flops 271579136 | bytes 9453568 | tf_op jit(solution)/shard_map/dot_general | solution.py:23
  172.6 3.6 %copy.71 = bf16[1,512,512]{2,0,1:T(2,128)(2,1)} copy(bf16[1,512,512]{1,2,0:T(8,128)(2,1)} %bitcast.90) | data formatting | bytes 1048576 | tf_op jit(solution)/shard_map/stack;reshape | solution.py:73
  176.2 3.0 %fusion.23 = bf16[4,512,128]{1,2,0:T(8,128)(2,1)} fusion(bf16[4,512,512]{1,2,0:T(8,128)(2,1)} %copy-done.6, bf16[512,4,128]{2,1,0:T(4,128)(2,1)} %copy-done.7), kind=kOutput, calls=%fused_computation.28 | convolution fusion | flops 268959744 | bytes 3145728 | tf_op jit(solution)/shard_map/dot_general | solution.py:23
  179.1 3.6 %copy.70 = bf16[1,512,512]{2,0,1:T(2,128)(2,1)} copy(bf16[1,512,512]{1,2,0:T(8,128)(2,1)} %bitcast.88) | data formatting | bytes 1048576 | tf_op jit(solution)/shard_map/stack;reshape | solution.py:73
  182.7 5.8 %pad_maximum_fusion = bf16[3,512,512]{2,0,1:T(4,128)(2,1)} fusion(bf16[1,512,512]{2,0,1:T(2,128)(2,1)S(1)} %copy.72, bf16[1,512,512]{2,0,1:T(2,128)(2,1)} %copy.71, bf16[1,512,512]{2,0,1:T(2,128)(2,1)} %copy.70), kind=kLoop, calls=%fused_computation.8 | loop fusion | flops 4718592 | bytes 3145728 | tf_op jit(solution)/shard_map/stack | solution.py:73
  188.5 4.8 %all-to-all-start.1 = ((bf16[3,512,512]{2,0,1:T(4,128)(2,1)}), bf16[3,512,512]{2,0,1:T(4,128)(2,1)}, u32[]{:S(2)}, u32[]{:S(2)}) async-start(bf16[3,512,512]{2,0,1:T(4,128)(2,1)} %pad_maximum_fusion), calls=%async_computation.3 | async-start | bytes 4194304 | tf_op jit(solution)/shard_map/all_to_all | solution.py:73
  193.3 3.3 %convolution_bitcast_fusion = f32[1,512,2048]{2,1,0:T(8,128)} fusion(bf16[512,512]{1,0:T(8,128)(2,1)S(1)} %copy-done.12, bf16[1,512,2048]{2,1,0:T(8,128)(2,1)S(1)} %copy-done.4), kind=kOutput, calls=%fused_computation.7 | convolution fusion | flops 1073741824 | bytes 6815744 | tf_op jit(solution)/shard_map/dot_general | solution.py:17
  198.5 19.8 %all-to-all-done.1 = bf16[3,512,512]{2,0,1:T(4,128)(2,1)} async-done(((bf16[3,512,512]{2,0,1:T(4,128)(2,1)}), bf16[3,512,512]{2,0,1:T(4,128)(2,1)}, u32[]{:S(2)}, u32[]{:S(2)}) %all-to-all-start.1) | async-done | bytes 1572896 | tf_op jit(solution)/shard_map/all_to_all | solution.py:73
  218.4 6.8 %fusion.49 = (bf16[1,128,4,512]{3,0,1,2:T(2,128)(2,1)S(1)}, bf16[1,128,4,512]{3,0,1,2:T(2,128)(2,1)}, bf16[1,128,4,512]{3,0,1,2:T(2,128)(2,1)S(1)}) fusion(bf16[3,128,4,512]{3,0,1,2:T(4,128)(2,1)} %bitcast.29), kind=kLoop, calls=%fused_computation.49 | loop fusion | bytes 3145728 | tf_op jit(solution)/shard_map/slice | solution.py:74
  228.8 2.7 %copy.74 = bf16[1,128,4,512]{3,2,1,0:T(4,128)(2,1)} copy(bf16[1,128,4,512]{3,0,1,2:T(2,128)(2,1)} %get-tuple-element.7) | data formatting | bytes 1048576 | tf_op jit(solution)/shard_map/slice | solution.py:74
  (68 shorter events, 38.6 us)
Async XLA Ops:
  7.2 70.1 %copy-start = (bf16[1,512,2048]{2,1,0:T(8,128)(2,1)S(1)}, bf16[1,512,2048]{2,1,0:T(8,128)(2,1)}, u32[]{:S(2)}) copy-start(bf16[1,512,2048]{2,1,0:T(8,128)(2,1)} %param.12) | copy-start | bytes 6291460
  14.2 36.5 %all-to-all-start = ((bf16[3,128,2048]{1,0,2:T(4,128)(2,1)}), bf16[3,128,2048]{1,0,2:T(4,128)(2,1)}, u32[]{:S(2)}, u32[]{:S(2)}) async-start(bf16[3,128,2048]{1,0,2:T(4,128)(2,1)} %copy.57), calls=%async_computation | async-start | bytes 4194304 | tf_op jit(solution)/shard_map/all_to_all | solution.py:45
  19.3 57.9 %all-gather.6.cloned.1.call-start = ((), (), s32[]{:S(2)}) async-start(), calls=%async_computation.7 | async-start | bytes 2621440 | tf_op jit(solution)/shard_map/all_gather | solution.py:43
  20.1 93.0 %reduce-scatter.3.cloned.1.call-start = ((), (), s32[]{:S(2)}) async-start(), calls=%async_computation.4 | async-start | bytes 2621440 | tf_op jit(solution)/shard_map/reduce_scatter | solution.py:57
  57.4 6.4 %copy-start.8 = (bf16[512,4,128]{2,1,0:T(4,128)(2,1)}, bf16[512,4,128]{2,1,0:T(4,128)(2,1)S(1)}, u32[]{:S(2)}) copy-start(bf16[512,4,128]{2,1,0:T(4,128)(2,1)S(1)} %reshape_squeeze.9) | copy-start | bytes 1572868
  58.7 8.4 %copy-start.7 = (bf16[512,4,128]{2,1,0:T(4,128)(2,1)}, bf16[512,4,128]{2,1,0:T(4,128)(2,1)S(1)}, u32[]{:S(2)}) copy-start(bf16[512,4,128]{2,1,0:T(4,128)(2,1)S(1)} %reshape_squeeze.10) | copy-start | bytes 1572868
  63.7 3.4 %copy-start.3 = (f32[4,512,512]{1,2,0:T(8,128)}, f32[4,512,512]{1,2,0:T(8,128)S(1)}, u32[]{:S(2)}) copy-start(f32[4,512,512]{1,2,0:T(8,128)S(1)} %fusion.32) | copy-start | bytes 12582916
  72.3 2.9 %copy-start.14 = (bf16[1,128,2048]{2,1,0:T(8,128)(2,1)S(1)}, bf16[1,128,2048]{2,1,0:T(8,128)(2,1)}, u32[]{:S(2)}) copy-start(bf16[1,128,2048]{2,1,0:T(8,128)(2,1)} %param.10) | copy-start | bytes 1572868
  77.2 73.6 %all-gather.4.cloned.1.call-start = ((), (), s32[]{:S(2)}) async-start(), calls=%async_computation.6 | async-start | bytes 2621440 | tf_op jit(solution)/shard_map/all_gather | solution.py:48
  80.2 2.0 collective-permute-start.1
  83.0 154.5 %reduce-scatter.5.cloned.1.call-start = ((), (), s32[]{:S(2)}) async-start(), calls=%async_computation.5 | async-start | bytes 2621440 | tf_op jit(solution)/shard_map/reduce_scatter | solution.py:62
  113.1 3.4 %copy-start.15 = (bf16[512,512]{1,0:T(8,128)(2,1)S(1)}, bf16[512,512]{1,0:T(8,128)(2,1)}, u32[]{:S(2)}) copy-start(bf16[512,512]{1,0:T(8,128)(2,1)} %reduce-scatter.3.cloned.1.call-done) | copy-start | bytes 1572868
  113.1 2.1 collective-permute-start
  115.2 1.5 copy-start.11
  116.7 34.1 %copy-start.4 = (bf16[1,512,2048]{2,1,0:T(8,128)(2,1)S(1)}, bf16[1,512,2048]{2,1,0:T(8,128)(2,1)}, u32[]{:S(2)}) copy-start(bf16[1,512,2048]{2,1,0:T(8,128)(2,1)} %all-gather.6.cloned.1.call-done) | copy-start | bytes 6291460
  150.8 3.9 %copy-start.10 = (bf16[1,512,2048]{2,1,0:T(8,128)(2,1)S(1)}, bf16[1,512,2048]{2,1,0:T(8,128)(2,1)}, u32[]{:S(2)}) copy-start(bf16[1,512,2048]{2,1,0:T(8,128)(2,1)} %param.11) | copy-start | bytes 6291460
  153.4 1.4 copy-start.5
  156.0 6.0 %copy-start.16 = (bf16[512,512]{0,1:T(8,128)(2,1)}, bf16[512,512]{0,1:T(8,128)(2,1)S(1)}, u32[]{:S(2)}) copy-start(bf16[512,512]{0,1:T(8,128)(2,1)S(1)} %fusion.15) | copy-start | bytes 1572868
  164.4 4.0 %copy-start.2 = (f32[4,512,512]{1,2,0:T(8,128)S(1)}, f32[4,512,512]{1,2,0:T(8,128)}, u32[]{:S(2)}) copy-start(f32[4,512,512]{1,2,0:T(8,128)} %get-tuple-element.13) | copy-start | bytes 12582916
  168.5 2.5 %copy-start.9 = (bf16[512,4,128]{2,1,0:T(4,128)(2,1)S(1)}, bf16[512,4,128]{2,1,0:T(4,128)(2,1)}, u32[]{:S(2)}) copy-start(bf16[512,4,128]{2,1,0:T(4,128)(2,1)} %copy-done.8) | copy-start | bytes 1572868
  169.6 1.3 copy-start.6
  188.5 4.8 %copy-start.12 = (bf16[512,512]{1,0:T(8,128)(2,1)S(1)}, bf16[512,512]{1,0:T(8,128)(2,1)}, u32[]{:S(2)}) copy-start(bf16[512,512]{1,0:T(8,128)(2,1)} %copy-done.11) | copy-start | bytes 1572868
  188.5 29.8 %all-to-all-start.1 = ((bf16[3,512,512]{2,0,1:T(4,128)(2,1)}), bf16[3,512,512]{2,0,1:T(4,128)(2,1)}, u32[]{:S(2)}, u32[]{:S(2)}) async-start(bf16[3,512,512]{2,0,1:T(4,128)(2,1)} %pad_maximum_fusion), calls=%async_computation.3 | async-start | bytes 4194304 | tf_op jit(solution)/shard_map/all_to_all | solution.py:73
  218.4 19.1 %copy-start.1 = (bf16[1,512,2048]{2,1,0:T(8,128)(2,1)S(1)}, bf16[1,512,2048]{2,1,0:T(8,128)(2,1)}, u32[]{:S(2)}) copy-start(bf16[1,512,2048]{2,1,0:T(8,128)(2,1)} %param.12) | copy-start | bytes 6291460
  (1 other events, 0.8 us)
Sparse Core Ops, SparseCore 0:
  22.0 48.1 all-gather.5
  77.3 35.6 reduce-scatter.2
  115.6 35.1 all-gather.3
  154.5 35.2 reduce-scatter.4

commit v2 on v1

v2 whole, which is shorter than its diff:
```python
import functools
import math

import jax
import jax.numpy as jnp
from jax import lax
from jax.experimental import pallas as pl
from jax.experimental.pallas import tpu as pltpu
from jax.sharding import PartitionSpec as P

HEAD = 128
ROWS = 256
BF16 = jnp.bfloat16
F32 = jnp.float32
MESH = pl.DeviceIdType.MESH
GM, Q, K, V, BACK, TERM, MIX, GQ, GK, GV, HID, KINDS = range(12)


def dot(left, right, left_dim, right_dim):
    return lax.dot_general(
        left, right, (((left_dim,), (right_dim,)), ((), ())), preferred_element_type=F32
    )


def kernel(
    n, q, k, v, hin, wo, wc, gm,
    mixed_o, gh_o, gq_o, gk_o, gv_o, gc_o,
    hq, hk, hv, gm_all, back, bc_all, att, wts, term, term_in, hid, hid_own,
    hg, gq, gk, gv, gk_acc, gv_acc, mix, mix_own, mix_in, send_sem, recv_sem,
):
    me = lax.axis_index("seq")
    mine = lax.axis_index("branch")
    other = 1 - mine
    tok, dim = gm.shape
    width = wc.shape[0]
    head_width = wo.shape[0]
    total = n * tok
    tile = min(ROWS, total)
    factor = 1.0 / math.sqrt(HEAD)

    def at(index, size):
        return pl.ds(pl.multiple_of(index * size, size), size)

    def to(step):
        return lax.rem(me + step, n)

    def source(step):
        return lax.rem(me - step + n, n)

    def copy(kind, step, src, dst, branch):
        return pltpu.make_async_remote_copy(
            src_ref=src,
            dst_ref=dst,
            send_sem=send_sem.at[kind, step],
            recv_sem=recv_sem.at[kind, step],
            device_id={"branch": branch, "seq": to(step)},
            device_id_type=MESH,
        )

    barrier = pltpu.get_barrier_semaphore()
    for step in range(n):
        pl.semaphore_signal(
            barrier, inc=1, device_id={"branch": other, "seq": to(step)}, device_id_type=MESH
        )
        if step:
            pl.semaphore_signal(
                barrier, inc=1, device_id={"branch": mine, "seq": to(step)}, device_id_type=MESH
            )
    pl.semaphore_wait(barrier, 2 * n - 1)

    gm_copies = [copy(GM, d, gm, gm_all.at[at(me, tok), :], mine) for d in range(1, n)]
    head_copies = [
        copy(kind, d, ref.at[:, at(to(d), head_width)], held.at[at(me, tok), :], mine)
        for kind, ref, held in ((Q, q, hq), (K, k, hk), (V, v, hv))
        for d in range(1, n)
    ]
    for c in gm_copies:
        c.start()
    for c in head_copies:
        c.start()
    gm_all[at(me, tok), :] = gm[...]
    for ref, held in ((q, hq), (k, hk), (v, hv)):
        held[at(me, tok), :] = ref[:, at(me, head_width)]

    for d in range(n):
        if d:
            gm_copies[d - 1].wait_recv()
        rows = at(source(d), tok)
        back[rows, :] = dot(gm_all[rows, :], wc[...], 1, 1).astype(BF16)
    back_copies = [
        copy(BACK, d, back, bc_all.at[:, at(me, width)], other) for d in range(n)
    ]
    for d in list(range(1, n)) + [0]:
        back_copies[d].start()

    for c in head_copies:
        c.wait_recv()

    def forward(index, carry):
        head = index // (total // tile)
        rows = at(index % (total // tile), tile)
        cols = at(head, HEAD)
        scores = dot(hq[rows, cols], hk[:, cols], 1, 1) * factor
        raised = jnp.exp(scores - jnp.max(scores, axis=-1, keepdims=True))
        weights = raised / jnp.sum(raised, axis=-1, keepdims=True)
        wts[head, rows, :] = weights
        att[rows, cols] = dot(weights.astype(BF16), hv[:, cols], 1, 0).astype(BF16)
        return carry

    heads = head_width // HEAD
    lax.fori_loop(0, heads * (total // tile), forward, 0)

    term_copies = [
        copy(TERM, d, term.at[:, at(to(d), width)], term_in.at[me], other) for d in range(n)
    ]
    own_rows = at(me, tok)
    for d in list(range(1, n)) + [0]:
        cols = at(to(d), width)

        def term_rows(index, carry, cols=cols):
            rows = at(index, tile)
            term[rows, cols] = dot(att[rows, :], wo[:, cols], 1, 0).astype(BF16)
            return carry

        lax.fori_loop(0, total // tile, term_rows, 0)
        term[own_rows, cols] = (
            dot(att[own_rows, :], wo[:, cols], 1, 0) + hin[:, cols].astype(F32)
        ).astype(BF16)
        term_copies[d].start()

    for c in back_copies:
        c.wait_recv()

    def head_grad(index, carry):
        rows = at(index, tok)
        grad = (gm_all[rows, :].astype(F32) + bc_all[rows, :].astype(F32)).astype(BF16)
        hg[rows, :] = dot(grad, wo[...], 1, 1).astype(BF16)
        return carry

    lax.fori_loop(0, n, head_grad, 0)
    gh_o[...] = (gm[...].astype(F32) + bc_all[own_rows, :].astype(F32)).astype(BF16)

    def backward(head, carry):
        cols = at(head, HEAD)
        for t in range(total // tile):
            rows = pl.ds(t * tile, tile)
            weights = wts[head, rows, :]
            grad = hg[rows, cols]
            grad_w = dot(grad, hv[:, cols], 1, 1)
            row_dot = jnp.sum(weights * grad_w, axis=-1, keepdims=True)
            d_scores = (weights * (grad_w - row_dot)).astype(BF16)
            gq[rows, cols] = (dot(d_scores, hk[:, cols], 1, 0) * factor).astype(BF16)
            part_k = dot(d_scores, hq[rows, cols], 0, 0)
            part_v = dot(weights.astype(BF16), grad, 0, 0)
            if t == 0:
                gk_acc[...] = part_k
                gv_acc[...] = part_v
            else:
                gk_acc[...] += part_k
                gv_acc[...] += part_v
        gk[:, cols] = (gk_acc[...] * factor).astype(BF16)
        gv[:, cols] = gv_acc[...].astype(BF16)
        return carry

    lax.fori_loop(0, heads, backward, 0)
    grads = ((GQ, gq, gq_o), (GK, gk, gk_o), (GV, gv, gv_o))
    grad_copies = [
        copy(kind, d, ref.at[at(to(d), tok), :], out.at[:, at(me, head_width)], mine)
        for kind, ref, out in grads
        for d in range(1, n)
    ]
    for c in grad_copies:
        c.start()
    for _, ref, out in grads:
        out[:, at(me, head_width)] = ref[own_rows, :]

    for c in term_copies:
        c.wait_recv()

    def add_terms(index, carry):
        rows = at(index, tok)
        summed = term_in[0, rows, :].astype(F32)
        for s in range(1, n):
            summed = summed + term_in[s, rows, :].astype(F32)
        hid[rows, :] = summed.astype(BF16)
        return carry

    lax.fori_loop(0, n, add_terms, 0)
    hid_copy = copy(HID, 0, hid, hid_own, other)
    hid_copy.start()
    mix_copies = [
        copy(MIX, d, mix.at[at(to(d), tok), :], mix_in.at[d - 1], mine) for d in range(1, n)
    ]
    own_cols = at(me, width)
    for d in list(range(1, n)) + [0]:
        rows = at(to(d), tok)
        mix_own[...] = dot(hid[rows, :], wc[...], 1, 0)
        if d == 1 or n == 1:
            hid_copy.wait_recv()
        mix_own[:, own_cols] += hid_own[rows, :].astype(F32)
        if d:
            mix[rows, :] = mix_own[...].astype(BF16)
            mix_copies[d - 1].start()

    def couple_grad(index, carry):
        cols = at(index, width)
        gc_o[:, cols] = dot(hid[...], gm_all[:, cols], 0, 0)
        return carry

    lax.fori_loop(0, dim // width, couple_grad, 0)
    for c in grad_copies:
        c.wait_recv()
    for c in mix_copies:
        c.wait_recv()
    summed = mix_own[...]
    for d in range(1, n):
        summed = summed + mix_in[d - 1].astype(F32)
    mixed_o[...] = summed.astype(BF16)
    for c in gm_copies + head_copies + back_copies + term_copies + grad_copies + mix_copies:
        c.wait_send()
    hid_copy.wait_send()


def on_device(queries, key_vecs, value_vecs, hidden_in, out_proj, couple_proj, grad_mixed):
    n = lax.axis_size("seq")
    tok, dim = grad_mixed.shape[1:]
    width = couple_proj.shape[1]
    head_width = out_proj.shape[1]
    wide = queries.shape[2]
    total = n * tok
    heads = head_width // HEAD
    item = pltpu.VMEM((total, head_width), BF16)
    whole = pltpu.VMEM((total, dim), BF16)
    slab = pltpu.VMEM((total, width), BF16)
    outs = pl.pallas_call(
        functools.partial(kernel, n),
        out_shape=[jax.ShapeDtypeStruct((tok, dim), BF16)] * 2
        + [jax.ShapeDtypeStruct((tok, wide), BF16)] * 3
        + [jax.ShapeDtypeStruct((width, dim), F32)],
        in_specs=[pl.BlockSpec(memory_space=pltpu.VMEM)] * 7,
        out_specs=[pl.BlockSpec(memory_space=pltpu.VMEM)] * 6,
        scratch_shapes=[
            item, item, item, whole, slab, whole, item,
            pltpu.VMEM((heads, total, total), F32),
            whole, pltpu.VMEM((n, total, width), BF16), slab, slab,
            item, item, item, item,
            pltpu.VMEM((total, HEAD), F32), pltpu.VMEM((total, HEAD), F32),
            whole, pltpu.VMEM((tok, dim), F32), pltpu.VMEM((max(n - 1, 1), tok, dim), BF16),
            pltpu.SemaphoreType.DMA((KINDS, n)), pltpu.SemaphoreType.DMA((KINDS, n)),
        ],
        compiler_params=pltpu.CompilerParams(
            collective_id=0, has_side_effects=True, vmem_limit_bytes=58 * 1024 * 1024
        ),
    )(
        queries[0], key_vecs[0], value_vecs[0], hidden_in[0], out_proj[0], couple_proj[0],
        grad_mixed[0],
    )
    return tuple(value[None] for value in outs)


def solution(mesh):
    token = P("branch", ("rep", "seq"), None)
    weight = P("branch", "seq", None)
    return jax.shard_map(
        on_device,
        mesh=mesh,
        in_specs=(token, token, token, token, weight, weight, token),
        out_specs=(token, token, token, token, token, P("branch", "seq", "rep")),
        check_vma=False,
    )
```

time: 245 us -> 149 us (0.61)
  Pallas kernels: 0 us -> 136 us
  waiting for transfers between devices: 117 us -> 0 us
  local copies, waits for them, and re-layouts: 50.9 us -> 11.6 us
  matrix products: 31.7 us -> 0 us
  other arithmetic: 19.5 us -> 0 us
  between operations: 14 us -> 0.65 us
  starting transfers between devices: 10.4 us -> 0 us
    pallas_call x0 -> x1, Pallas kernels: none -> 136 us  [on_device(): pl.pallas_call(functools.partial(kernel, n), out_shape=[jax.ShapeDtypeStr...]
    all_to_all x2 -> x0, waiting for transfers between devices: 50.4 us -> none  [the longest x1 30.6 us: on_device(): lax.all_to_all(stacked, 'seq', split_axis=2, concat_axis=1, tiled=True)]
    all_gather x2 -> x0, waiting for transfers between devices: 32.4 us -> none  [the longest x1 32.4 us: on_device(): lax.all_gather(swapped(back, 'branch'), 'seq', axis=1, tiled=True)]
    dot_general x11 -> x0, matrix products: 31.7 us -> none  [the longest x6 20.1 us: batched(): lax.dot_general(left, right, (((left_dim,), (right_dim,)), ((0,), (0,))),...]
    reduce_scatter x2 -> x0, waiting for transfers between devices: 29.9 us -> none  [the longest x1 29.9 us: on_device(): hidden = lax.psum_scatter(term, 'seq', scatter_dimension=1, tiled=True)]
    slice x8 -> x0, local copies, waits for them, and re-layouts: 21.5 us -> none  [the longest x3 10.5 us: on_device(): out[2:3]]
    another operation x7 -> x0, local copies, waits for them, and re-layouts: 15.3 us -> none  [the longest x3 9.55 us: on_device(): jnp.stack([gq, gk, gv])]
    all_to_all x2 -> x0, starting transfers between devices: 9.97 us -> none  [the longest x1 5.16 us: on_device(): lax.all_to_all(stacked, 'seq', split_axis=2, concat_axis=1, tiled=True)]
  transfers between devices with their start and end apart: 8 -> 0, of which waited for: 6 -> 0; matrix products, arithmetic and copies ran while one was open for 37% -> 0% of each run, Pallas kernels for 0% -> 0%
where the time goes in v2:
time: 149 us; the launch traced here: 148 us
  Pallas kernels  136 us (91%)
  local copies, waits for them, and re-layouts  11.6 us (8%)
    pallas_call x1, Pallas kernels, on_device(): pl.pallas_call(functools.partial(kernel, n), out_shape=[jax.ShapeDtypeStr...  136 us
    unnamed x8, local copies, waits for them, and re-layouts  11.6 us

profile of v2, /device:TPU:0, one launch (start us, length us, event | category | flops | bytes accessed | tf_op | source)
XLA Modules:
  0.0 148.4 jit_solution(4799113104055634832)
XLA Ops:
  0.6 136.2 %shard_map.118 = (bf16[128,2048]{1,0:T(8,128)(2,1)}, bf16[128,2048]{1,0:T(8,128)(2,1)}, bf16[128,2048]{1,0:T(8,128)(2,1)}, bf16[128,2048]{1,0:T(8,128)(2,1)}, bf...) custom-call(bf16[128,2048]{1,0:T(8,128)(2,1)} %bitcast.21, bf16[128,2048]{1,0:T(8,128)(2,1)} %bitcast.22, ...), custom_call_target="tpu_custom_call" | custom-call | tf_op jit(solution)/shard_map/pallas_call | solution.py:235
  136.8 0.0 copy-start
  136.8 2.0 %copy.19 = bf16[1,128,2048]{2,1,0:T(8,128)(2,1)} copy(bf16[1,128,2048]{2,1,0:T(8,128)(2,1)} %bitcast.20) | data formatting | bytes 1048576
  138.9 1.9 %copy.20 = bf16[1,128,2048]{2,1,0:T(8,128)(2,1)} copy(bf16[1,128,2048]{2,1,0:T(8,128)(2,1)} %bitcast.19) | data formatting | bytes 1048576
  140.7 1.9 %copy.21 = bf16[1,128,2048]{2,1,0:T(8,128)(2,1)} copy(bf16[1,128,2048]{2,1,0:T(8,128)(2,1)} %bitcast.18) | data formatting | bytes 1048576
  142.6 1.9 %copy.22 = bf16[1,128,2048]{2,1,0:T(8,128)(2,1)} copy(bf16[1,128,2048]{2,1,0:T(8,128)(2,1)} %bitcast.17) | data formatting | bytes 1048576
  144.5 1.9 %copy.23 = bf16[1,128,2048]{2,1,0:T(8,128)(2,1)} copy(bf16[1,128,2048]{2,1,0:T(8,128)(2,1)} %bitcast.16) | data formatting | bytes 1048576
  146.4 0.0 copy-done
  146.4 2.0 %copy.24 = f32[1,512,2048]{2,1,0:T(8,128)} copy(f32[1,512,2048]{2,1,0:T(8,128)S(1)} %bitcast.13) | data formatting | bytes 8388608
Async XLA Ops:
  136.8 9.6 %copy-start = (f32[512,2048]{1,0:T(8,128)S(1)}, f32[512,2048]{1,0:T(8,128)}, u32[]{:S(2)}) copy-start(f32[512,2048]{1,0:T(8,128)} %get-tuple-element.17) | copy-start | bytes 12582916

commit v3 on v2

--- a/solution.py
+++ b/solution.py
@@ -10,6 +10,7 @@
 
 HEAD = 128
 ROWS = 256
+PIECES = 4
 BF16 = jnp.bfloat16
 F32 = jnp.float32
 MESH = pl.DeviceIdType.MESH
@@ -23,10 +24,11 @@
 
 
 def kernel(
-    n, q, k, v, hin, wo, wc, gm,
-    mixed_o, gh_o, gq_o, gk_o, gv_o, gc_o,
+    n, q, k, v, hin, wo_hbm, wc_hbm, gm,
+    mixed_o, gh_o, gq_o, gk_o, gv_o, gc_hbm,
     hq, hk, hv, gm_all, back, bc_all, att, wts, term, term_in, hid, hid_own,
-    hg, gq, gk, gv, gk_acc, gv_acc, mix, mix_own, mix_in, send_sem, recv_sem,
+    hg, gq, gk, gv, gk_acc, gv_acc, mix, mix_own, mix_in, wo, wc, gc_o,
+    send_sem, recv_sem, load_sem,
 ):
     me = lax.axis_index("seq")
     mine = lax.axis_index("branch")
@@ -74,26 +76,21 @@
         for kind, ref, held in ((Q, q, hq), (K, k, hk), (V, v, hv))
         for d in range(1, n)
     ]
-    for c in gm_copies:
-        c.start()
     for c in head_copies:
         c.start()
+    wo_load = pltpu.make_async_copy(wo_hbm, wo, load_sem.at[0])
+    wc_load = pltpu.make_async_copy(wc_hbm, wc, load_sem.at[1])
+    wo_load.start()
+    wc_load.start()
     gm_all[at(me, tok), :] = gm[...]
     for ref, held in ((q, hq), (k, hk), (v, hv)):
         held[at(me, tok), :] = ref[:, at(me, head_width)]
 
-    for d in range(n):
-        if d:
-            gm_copies[d - 1].wait_recv()
-        rows = at(source(d), tok)
-        back[rows, :] = dot(gm_all[rows, :], wc[...], 1, 1).astype(BF16)
-    back_copies = [
-        copy(BACK, d, back, bc_all.at[:, at(me, width)], other) for d in range(n)
-    ]
-    for d in list(range(1, n)) + [0]:
-        back_copies[d].start()
-
-    for c in head_copies:
+    for c in head_copies[: 2 * (n - 1)]:
+        c.wait_recv()
+    for c in gm_copies:
+        c.start()
+    for c in head_copies[2 * (n - 1) :]:
         c.wait_recv()
 
     def forward(index, carry):
@@ -110,6 +107,7 @@
     heads = head_width // HEAD
     lax.fori_loop(0, heads * (total // tile), forward, 0)
 
+    wo_load.wait()
     term_copies = [
         copy(TERM, d, term.at[:, at(to(d), width)], term_in.at[me], other) for d in range(n)
     ]
@@ -128,8 +126,49 @@
         ).astype(BF16)
         term_copies[d].start()
 
+    wc_load.wait()
+    for d in range(n):
+        if d:
+            gm_copies[d - 1].wait_recv()
+        rows = at(source(d), tok)
+        back[rows, :] = dot(gm_all[rows, :], wc[...], 1, 1).astype(BF16)
+    back_copies = [
+        copy(BACK, d, back, bc_all.at[:, at(me, width)], other) for d in range(n)
+    ]
+    for d in list(range(1, n)) + [0]:
+        back_copies[d].start()
+
+    for c in term_copies:
+        c.wait_recv()
+
+    def add_terms(index, carry):
+        rows = at(index, tok)
+        summed = term_in[0, rows, :].astype(F32)
+        for s in range(1, n):
+            summed = summed + term_in[s, rows, :].astype(F32)
+        hid[rows, :] = summed.astype(BF16)
+        return carry
+
+    lax.fori_loop(0, n, add_terms, 0)
+    hid_copy = copy(HID, 0, hid, hid_own, other)
+    hid_copy.start()
+    mix_copies = [
+        copy(MIX, d, mix.at[at(to(d), tok), :], mix_in.at[d - 1], mine) for d in range(1, n)
+    ]
+    own_cols = at(me, width)
+    for d in list(range(1, n)) + [0]:
+        rows = at(to(d), tok)
+        mix_own[...] = dot(hid[rows, :], wc[...], 1, 0)
+        if d == 1 or n == 1:
+            hid_copy.wait_recv()
+        mix_own[:, own_cols] += hid_own[rows, :].astype(F32)
+        if d:
+            mix[rows, :] = mix_own[...].astype(BF16)
+
     for c in back_copies:
         c.wait_recv()
+    for c in mix_copies:
+        c.start()
 
     def head_grad(index, carry):
         rows = at(index, tok)
@@ -174,51 +213,45 @@
     for _, ref, out in grads:
         out[:, at(me, head_width)] = ref[own_rows, :]
 
-    for c in term_copies:
-        c.wait_recv()
-
-    def add_terms(index, carry):
-        rows = at(index, tok)
-        summed = term_in[0, rows, :].astype(F32)
-        for s in range(1, n):
-            summed = summed + term_in[s, rows, :].astype(F32)
-        hid[rows, :] = summed.astype(BF16)
-        return carry
-
-    lax.fori_loop(0, n, add_terms, 0)
-    hid_copy = copy(HID, 0, hid, hid_own, other)
-    hid_copy.start()
-    mix_copies = [
-        copy(MIX, d, mix.at[at(to(d), tok), :], mix_in.at[d - 1], mine) for d in range(1, n)
-    ]
-    own_cols = at(me, width)
-    for d in list(range(1, n)) + [0]:
-        rows = at(to(d), tok)
-        mix_own[...] = dot(hid[rows, :], wc[...], 1, 0)
-        if d == 1 or n == 1:
-            hid_copy.wait_recv()
-        mix_own[:, own_cols] += hid_own[rows, :].astype(F32)
-        if d:
-            mix[rows, :] = mix_own[...].astype(BF16)
-            mix_copies[d - 1].start()
-
     def couple_grad(index, carry):
         cols = at(index, width)
         gc_o[:, cols] = dot(hid[...], gm_all[:, cols], 0, 0)
         return carry
 
     lax.fori_loop(0, dim // width, couple_grad, 0)
-    for c in grad_copies:
-        c.wait_recv()
+    gc_store = pltpu.make_async_copy(gc_o, gc_hbm, load_sem.at[2])
+    gc_store.start()
     for c in mix_copies:
         c.wait_recv()
     summed = mix_own[...]
     for d in range(1, n):
         summed = summed + mix_in[d - 1].astype(F32)
     mixed_o[...] = summed.astype(BF16)
+    for c in grad_copies:
+        c.wait_recv()
     for c in gm_copies + head_copies + back_copies + term_copies + grad_copies + mix_copies:
         c.wait_send()
     hid_copy.wait_send()
+    gc_store.wait()
+
+
+def store_kernel(*refs):
+    sems = refs[-1]
+    copies = []
+    for index in range(5):
+        copies.append((refs[index], refs[index + 6]))
+    rows = refs[5].shape[0] // PIECES
+    for piece in range(PIECES):
+        part = pl.ds(piece * rows, rows)
+        copies.append((refs[5].at[part, :], refs[11].at[part, :]))
+    copies = [
+        pltpu.make_async_copy(src, dst, sems.at[index])
+        for index, (src, dst) in enumerate(copies)
+    ]
+    for c in copies:
+        c.start()
+    for c in copies:
+        c.wait()
 
 
 def on_device(queries, key_vecs, value_vecs, hidden_in, out_proj, couple_proj, grad_mixed):
@@ -232,13 +265,15 @@
     item = pltpu.VMEM((total, head_width), BF16)
     whole = pltpu.VMEM((total, dim), BF16)
     slab = pltpu.VMEM((total, width), BF16)
+    vmem = pl.BlockSpec(memory_space=pltpu.VMEM)
+    hbm = pl.BlockSpec(memory_space=pl.ANY)
     outs = pl.pallas_call(
         functools.partial(kernel, n),
         out_shape=[jax.ShapeDtypeStruct((tok, dim), BF16)] * 2
         + [jax.ShapeDtypeStruct((tok, wide), BF16)] * 3
         + [jax.ShapeDtypeStruct((width, dim), F32)],
-        in_specs=[pl.BlockSpec(memory_space=pltpu.VMEM)] * 7,
-        out_specs=[pl.BlockSpec(memory_space=pltpu.VMEM)] * 6,
+        in_specs=[vmem] * 4 + [hbm] * 2 + [vmem],
+        out_specs=[vmem] * 5 + [hbm],
         scratch_shapes=[
             item, item, item, whole, slab, whole, item,
             pltpu.VMEM((heads, total, total), F32),
@@ -246,7 +281,10 @@
             item, item, item, item,
             pltpu.VMEM((total, HEAD), F32), pltpu.VMEM((total, HEAD), F32),
             whole, pltpu.VMEM((tok, dim), F32), pltpu.VMEM((max(n - 1, 1), tok, dim), BF16),
+            pltpu.VMEM((head_width, dim), BF16), pltpu.VMEM((width, dim), BF16),
+            pltpu.VMEM((width, dim), F32),
             pltpu.SemaphoreType.DMA((KINDS, n)), pltpu.SemaphoreType.DMA((KINDS, n)),
+            pltpu.SemaphoreType.DMA((3,)),
         ],
         compiler_params=pltpu.CompilerParams(
             collective_id=0, has_side_effects=True, vmem_limit_bytes=58 * 1024 * 1024
@@ -255,6 +293,13 @@
         queries[0], key_vecs[0], value_vecs[0], hidden_in[0], out_proj[0], couple_proj[0],
         grad_mixed[0],
     )
+    outs = pl.pallas_call(
+        store_kernel,
+        out_shape=[jax.ShapeDtypeStruct(value.shape, value.dtype) for value in outs],
+        in_specs=[hbm] * 6,
+        out_specs=[hbm] * 6,
+        scratch_shapes=[pltpu.SemaphoreType.DMA((5 + PIECES,))],
+    )(*outs)
     return tuple(value[None] for value in outs)
 
 

time: 149 us -> 344 us (2.31)
  Pallas kernels: 136 us -> 343 us
  local copies, waits for them, and re-layouts: 11.6 us -> 0 us
    pallas_call x0 -> x1, Pallas kernels: none -> 208 us  [on_device(): pl.pallas_call(store_kernel, out_shape=[jax.ShapeDtypeStruct(value.shape,...]
    unnamed x8 -> x0, local copies, waits for them, and re-layouts: 11.6 us -> none
where the time goes in v3:
time: 344 us
  Pallas kernels  343 us (100%)
    pallas_call x1, Pallas kernels, on_device(): pl.pallas_call(store_kernel, out_shape=[jax.ShapeDtypeStruct(value.shape,...  208 us
    pallas_call x1, Pallas kernels, on_device(): pl.pallas_call(functools.partial(kernel, n), out_shape=[jax.ShapeDtypeStr...  136 us

profile of v3, /device:TPU:0, one launch (start us, length us, event | category | flops | bytes accessed | tf_op | source)
XLA Modules:
  0.0 343.9 jit_solution(18104426960020971671)
XLA Ops:
  0.6 135.6 %shard_map.118 = (bf16[128,2048]{1,0:T(8,128)(2,1)}, bf16[128,2048]{1,0:T(8,128)(2,1)}, bf16[128,2048]{1,0:T(8,128)(2,1)}, bf16[128,2048]{1,0:T(8,128)(2,1)}, bf...) custom-call(bf16[128,2048]{1,0:T(8,128)(2,1)} %bitcast.15, bf16[128,2048]{1,0:T(8,128)(2,1)} %bitcast.16, ...), custom_call_target="tpu_custom_call" | custom-call | tf_op jit(solution)/shard_map/pallas_call | solution.py:270
  136.2 207.7 %shard_map.119 = (bf16[128,2048]{1,0:T(8,128)(2,1)}, bf16[128,2048]{1,0:T(8,128)(2,1)}, bf16[128,2048]{1,0:T(8,128)(2,1)}, bf16[128,2048]{1,0:T(8,128)(2,1)}, bf...) custom-call(bf16[128,2048]{1,0:T(8,128)(2,1)} %get-tuple-element.18.refs_0_, bf16[128,2048]{1,0:T(8,128)(2,1)} %get-tuple-element.19.refs_1_, ...), custom_call_target="tpu_custom_call" | custom-call | tf_op jit(solution)/shard_map/pallas_call | solution.py:296

commit v4 on v3

--- a/solution.py
+++ b/solution.py
@@ -236,21 +236,29 @@
 
 
 def store_kernel(*refs):
-    sems = refs[-1]
-    copies = []
-    for index in range(5):
-        copies.append((refs[index], refs[index + 6]))
+    values, outs, held = refs[:6], refs[6:12], refs[12:18]
+    load_sem, store_sem = refs[18:]
+    blocks = [(index, pl.ds(0, refs[index].shape[0])) for index in range(5)]
     rows = refs[5].shape[0] // PIECES
-    for piece in range(PIECES):
-        part = pl.ds(piece * rows, rows)
-        copies.append((refs[5].at[part, :], refs[11].at[part, :]))
-    copies = [
-        pltpu.make_async_copy(src, dst, sems.at[index])
-        for index, (src, dst) in enumerate(copies)
-    ]
-    for c in copies:
-        c.start()
-    for c in copies:
+    blocks += [(5, pl.ds(piece * rows, rows)) for piece in range(PIECES)]
+    loads, stores = [], []
+    for place, (index, part) in enumerate(blocks):
+        loads.append(
+            pltpu.make_async_copy(
+                values[index].at[part, :], held[index].at[part, :], load_sem.at[place]
+            )
+        )
+        stores.append(
+            pltpu.make_async_copy(
+                held[index].at[part, :], outs[index].at[part, :], store_sem.at[place]
+            )
+        )
+    for c in loads:
+        c.start()
+    for load, store in zip(loads, stores):
+        load.wait()
+        store.start()
+    for c in stores:
         c.wait()
 
 
@@ -298,7 +306,9 @@
         out_shape=[jax.ShapeDtypeStruct(value.shape, value.dtype) for value in outs],
         in_specs=[hbm] * 6,
         out_specs=[hbm] * 6,
-        scratch_shapes=[pltpu.SemaphoreType.DMA((5 + PIECES,))],
+        scratch_shapes=[pltpu.VMEM(value.shape, value.dtype) for value in outs]
+        + [pltpu.SemaphoreType.DMA((5 + PIECES,))] * 2,
+        compiler_params=pltpu.CompilerParams(vmem_limit_bytes=24 * 1024 * 1024),
     )(*outs)
     return tuple(value[None] for value in outs)
 

time: 344 us -> 148 us (0.43)
  Pallas kernels: 343 us -> 139 us
  local copies, waits for them, and re-layouts: 0 us -> 7.39 us
    pallas_call x1, Pallas kernels: 208 us -> 3.45 us  [on_device(): pl.pallas_call(store_kernel, out_shape=[jax.ShapeDtypeStruct(value.shape,...]
    unnamed x0 -> x12, local copies, waits for them, and re-layouts: none -> 7.39 us
where the time goes in v4:
time: 148 us; the launch traced here: 147 us
  Pallas kernels  139 us (94%)
  local copies, waits for them, and re-layouts  7.39 us (5%)
    pallas_call x1, Pallas kernels, on_device(): pl.pallas_call(functools.partial(kernel, n), out_shape=[jax.ShapeDtypeStr...  136 us
    unnamed x12, local copies, waits for them, and re-layouts  7.39 us
    pallas_call x1, Pallas kernels, on_device(): pl.pallas_call(store_kernel, out_shape=[jax.ShapeDtypeStruct(value.shape,...  3.45 us

profile of v4, /device:TPU:0, one launch (start us, length us, event | category | flops | bytes accessed | tf_op | source)
XLA Modules:
  0.0 147.1 jit_solution(4804047970208169060)
XLA Ops:
  0.6 135.6 %shard_map.118 = (bf16[128,2048]{1,0:T(8,128)(2,1)}, bf16[128,2048]{1,0:T(8,128)(2,1)}, bf16[128,2048]{1,0:T(8,128)(2,1)}, bf16[128,2048]{1,0:T(8,128)(2,1)}, bf...) custom-call(bf16[128,2048]{1,0:T(8,128)(2,1)} %bitcast.15, bf16[128,2048]{1,0:T(8,128)(2,1)} %bitcast.16, ...), custom_call_target="tpu_custom_call" | custom-call | tf_op jit(solution)/shard_map/pallas_call | solution.py:278
  136.2 0.0 copy-start
  136.3 2.2 %copy-done = f32[512,2048]{1,0:T(8,128)S(1)} copy-done((f32[512,2048]{1,0:T(8,128)S(1)}, f32[512,2048]{1,0:T(8,128)}, u32[]{:S(2)}) %copy-start) | copy-done | bytes 4194328
  138.4 0.0 copy-start.1
  138.4 1.0 copy-done.1
  139.5 0.0 copy-start.2
  139.5 1.0 copy-done.2
  140.5 0.0 copy-start.3
  140.5 1.0 copy-done.3
  141.6 0.0 copy-start.4
  141.6 1.0 copy-done.4
  142.6 0.0 copy-start.5
  142.6 1.0 copy-done.5
  143.6 3.5 %shard_map.119 = (bf16[128,2048]{1,0:T(8,128)(2,1)}, bf16[128,2048]{1,0:T(8,128)(2,1)}, bf16[128,2048]{1,0:T(8,128)(2,1)}, bf16[128,2048]{1,0:T(8,128)(2,1)}, bf...) custom-call(bf16[128,2048]{1,0:T(8,128)(2,1)S(1)} %copy-done.1, bf16[128,2048]{1,0:T(8,128)(2,1)S(1)} %copy-done.2, ...), custom_call_target="tpu_custom_call" | custom-call | tf_op jit(solution)/shard_map/pallas_call | solution.py:304
Async XLA Ops:
  136.2 2.2 %copy-start = (f32[512,2048]{1,0:T(8,128)S(1)}, f32[512,2048]{1,0:T(8,128)}, u32[]{:S(2)}) copy-start(f32[512,2048]{1,0:T(8,128)} %get-tuple-element.23.refs_5_) | copy-start | bytes 12582916
  138.4 1.0 copy-start.1
  139.5 1.0 copy-start.2
  140.5 1.0 copy-start.3
  141.6 1.0 copy-start.4
  142.6 1.0 copy-start.5
